TPU v7x, 32 devices: a whole 2x2x4 slice. The times are simulated.
32 devices in a mesh: section: 2 (over x), ctx: 4 (over z), mp: 4 (over y, core).
Axes of the slice: x: 2, y: 2, z: 4, core: 2. Of those that a mesh axis runs over, the one named last changes fastest.
Arguments:
- queries: bfloat16 [2, 1024, 4096], P('section', 'ctx', 'mp'), may hold values from -130 to 130
- keys: bfloat16 [2, 1024, 512], P('section', 'ctx', 'mp'), may hold values from -4.5 to 4.5
- values: bfloat16 [2, 1024, 512], P('section', 'ctx', 'mp'), may hold values from -6 to 6
- doc_lengths: int32 [2, 16], P('section'), may hold values from 1 to 512, 1024 in all within a row
Outputs:
- attended: bfloat16 [2, 1024, 4096], P('section', ('ctx', 'mp'))
- passed: bfloat16 [2, 1024, 4096], P('section', ('ctx', 'mp'))
All inputs are finite; a program needn't handle non-finite values.
Results may differ from a plain program's by a relative error of at most 0.004.
Values may be sent and summed in bfloat16 or wider, within the bound.
A program may use at most 192 MiB of HBM per device.

v0:
```python
import math

import jax
import jax.numpy as jnp
from jax import lax
from jax.sharding import PartitionSpec as P

DH = 128
DOCS = 16


def from_behind(block, axis, distance):
    devices = range(lax.axis_size(axis))
    route = [((i - distance) % len(devices), i) for i in devices]
    return lax.ppermute(block, axis, route)


def doc_of(positions, ends):
    return jnp.sum((positions[:, None] >= ends[None, :]).astype(jnp.int32), axis=1)


def body(queries, keys, values, doc_lengths):
    query_rows = queries[0]
    key_rows = keys[0]
    value_rows = values[0]
    lengths = doc_lengths[0]
    rows = query_rows.shape[0]
    kv_heads = key_rows.shape[1] // DH
    heads = query_rows.shape[1] // DH
    group = heads // kv_heads
    cycle = lax.axis_size("ctx")
    base_len = rows * cycle // 16
    position = lax.axis_index("ctx")
    first = position * rows
    ends = jnp.cumsum(lengths)
    query_pos = first + jnp.arange(rows, dtype=jnp.int32)
    query_doc = doc_of(query_pos, ends)
    lookup = query_doc[:, None] == jnp.arange(DOCS, dtype=jnp.int32)[None, :]
    query_len = jnp.sum(jnp.where(lookup, lengths[None, :], 0), axis=1).astype(jnp.float32)
    factor = jnp.maximum(1.0, jnp.log(query_len) / math.log(float(base_len))) * (
        1.0 / math.sqrt(DH)
    )
    query_heads = query_rows.reshape(rows, kv_heads, group, DH)
    key_piece = lax.all_gather(key_rows, "ctx", axis=0, tiled=True)
    value_piece = lax.all_gather(value_rows, "ctx", axis=0, tiled=True)
    top = jnp.full((kv_heads, group, rows), -1e30, jnp.float32)
    count = key_piece.shape[0]
    key_pos = jnp.arange(count, dtype=jnp.int32)
    key_doc = doc_of(key_pos, ends)
    score = jnp.einsum(
        "qhgd,khd->hgqk",
        query_heads,
        key_piece.reshape(count, kv_heads, DH),
        preferred_element_type=jnp.float32,
    )
    score = score * factor[None, None, :, None]
    allowed = (
        (query_doc[:, None] == key_doc[None, :])
        & (key_pos[None, :] <= query_pos[:, None])
        & (key_pos[None, :] >= 0)
    )
    score = jnp.where(allowed[None, None], score, -1e30)
    new_top = jnp.maximum(top, jnp.max(score, axis=-1))
    weight = jnp.where(allowed[None, None], jnp.exp(score - new_top[..., None]), 0.0)
    total = jnp.sum(weight, axis=-1)
    update = jnp.einsum(
        "hgqk,khd->qhgd",
        weight.astype(jnp.bfloat16),
        value_piece.reshape(count, kv_heads, DH),
        preferred_element_type=jnp.float32,
    )
    summed = update
    top, total, summed = (new_top, total, summed)
    result = summed / jnp.transpose(total, (2, 0, 1))[..., None]
    result = result.astype(jnp.bfloat16).reshape(rows, heads * DH)
    own = lax.all_to_all(result, "mp", split_axis=0, concat_axis=1, tiled=True)
    moved = from_behind(own, "section", 1)
    return (own[None], moved[None])


def solution(mesh):
    return jax.shard_map(
        body,
        mesh=mesh,
        in_specs=(
            P("section", "ctx", "mp"),
            P("section", "ctx", "mp"),
            P("section", "ctx", "mp"),
            P("section", None),
        ),
        out_specs=(P("section", ("ctx", "mp"), None), P("section", ("ctx", "mp"), None)),
        check_vma=False,
    )
```

profile of v0, /device:TPU:0, one launch (start us, length us, event | category | flops | bytes accessed | tf_op | source)
XLA Modules:
  0.0 66.4 jit_solution(4049901999660630585)
XLA Ops:
  0.6 0.0 copy-start
  0.6 0.8 %copy.19 = s32[16,1]{1,0:T(8,128)S(1)} copy(s32[16,1]{0,1:T(1,128)} %bitcast.86) | data formatting | bytes 128 | tf_op jit(solution)/shard_map/reshape.113
  1.4 0.1 reduce.2
  1.6 0.1 convert_reduce_fusion
  1.7 0.1 convert_reduce_fusion.1
  1.7 0.2 fusion.10
  2.0 0.7 %select_reduce_fusion = s32[256]{0:T(256)S(1)} fusion(s32[16]{0:T(128)} %bitcast.87, s32[256]{0:T(256)S(1)} %convert_reduce_fusion.1), kind=kLoop, calls=%fused_computation.19 | loop fusion | flops 12032 | bytes 2112 | tf_op jit(solution)/shard_map/reduce_sum | solution.py:39
  2.8 1.1 %copy.27 = bf16[32,8,8,128]{3,2,1,0:T(8,128)(2,1)S(1)} copy(bf16[32,8,8,128]{3,1,2,0:T(8,128)(2,1)} %bitcast.82) | data formatting | bytes 1048576
  3.9 15.8 %all-gather = bf16[1,1024,128]{2,1,0:T(8,128)(2,1)S(1)} all-gather(bf16[1,256,128]{2,1,0:T(8,128)(2,1)} %param.5), channel_id=2, replica_groups=mesh['section'=2,'ctx'=4,'mp'=4] {'ctx'}, dimensions={1}, use_global_device_ids=true | all-gather | bytes 327680 | tf_op jit(solution)/shard_map/all_gather | solution.py:44
  19.7 1.4 %fusion = (f32[8,256]{1,0:T(8,128)S(1)}, f32[1024,256,8]{1,0,2:T(8,128)S(1)}) fusion(f32[256]{0:T(256)S(1)} %maximum_multiply_fusion, pred[256,1024]{0,1:T(8,128)(4,1)S(1)} %fusion.10, bf16[256,8,128]{2,1,0:T(8,128)(2,1)S(1)} %bitcast.81, bf16[1,1024,128]{2,1,0:T(8,128)(2,1)S(1)} %all-gather), kind=kOutput, calls=%fused_computation.3 | convolution fusion | flops 543160320 | bytes 9446400 | tf_op jit(solution)/shard_map/qhgd,khd->hgqk/dot_general | solution.py:50
  21.1 0.0 copy-done
  21.1 14.4 %all-gather.1 = bf16[1,1024,128]{2,1,0:T(8,128)(2,1)S(1)} all-gather(bf16[1,256,128]{2,1,0:T(8,128)(2,1)S(1)} %copy-done), channel_id=3, replica_groups=mesh['section'=2,'ctx'=4,'mp'=4] {'ctx'}, dimensions={1}, use_global_device_ids=true | all-gather | bytes 327680 | tf_op jit(solution)/shard_map/all_gather | solution.py:45
  35.6 2.0 %fusion.1 = f32[8,256]{1,0:T(8,128)S(1)} fusion(f32[1024,256,8]{1,0,2:T(8,128)S(1)} %get-tuple-element.3, f32[8,256]{1,0:T(8,128)S(1)} %broadcast_maximum_fusion, f32[256]{0:T(256)S(1)} %maximum_multiply_fusion, pred[256,1024]{0,1:T(8,128)(4,1)S(1)} %fusion.10), kind=kLoop, calls=%fused_computation.4 | loop fusion | flops 10483712 | bytes 8668160 | tf_op jit(solution)/shard_map/reduce_sum | solution.py:65
  37.6 2.6 %divide_convert_fusion = bf16[256,1,8,128]{3,0,2,1:T(8,128)(2,1)S(1)} fusion(f32[1024,256,8]{1,0,2:T(8,128)S(1)} %get-tuple-element.3, f32[8,256]{1,0:T(8,128)S(1)} %broadcast_maximum_fusion, f32[256]{0:T(256)S(1)} %maximum_multiply_fusion, pred[256,1024]{0,1:T(8,128)(4,1)S(1)} %fusion.10, f32[256,8]{0,1:T(8,128)S(1)} %bitcast.85, ...), kind=kOutput, calls=%fused_computation.10 | convolution fusion | flops 547880960 | bytes 9454592 | tf_op jit(solution)/shard_map/hgqk,khd->qhgd/dot_general | solution.py:66
  40.2 0.3 copy.22
  40.6 0.2 all_to_all.14
  40.8 11.4 %all_to_all.19 = bf16[4,64,1024]{2,1,0:T(8,128)(2,1)S(1)} all-to-all(bf16[4,64,1024]{2,1,0:T(8,128)(2,1)S(1)} %all_to_all.14), channel_id=1, replica_groups=mesh['section'=2,'ctx'=4,'mp'=4] {'mp'}, dimensions={0} | all-to-all | bytes 1048576 | tf_op jit(solution)/shard_map/all_to_all | solution.py:76
  52.3 1.6 %collective-permute-start = (bf16[64,4096]{1,0:T(8,128)(2,1)S(1)}, bf16[64,4096]{1,0:T(8,128)(2,1)S(1)}, u32[]{:S(2)}, u32[]{:S(2)}) collective-permute-start(bf16[64,4096]{1,0:T(8,128)(2,1)S(1)} %bitcast.84), channel_id=1, source_target_pairs={{16,0},{0,16},{17,1},{1,17},{18,2},{2,18},{19,3},{3,19},{20,4},{4,... | collective-permute-start | bytes 1572872 | tf_op jit(solution)/shard_map/ppermute | solution.py:15
  53.8 0.4 copy.23
  54.3 1.2 %broadcast_in_dim.64 = bf16[1,64,4096]{2,1,0:T(8,128)(2,1)} reshape(bf16[64,4,1024]{2,1,0:T(4,128)(2,1)S(1)} %copy.23) | data formatting | bytes 1048576 | tf_op jit(solution)/shard_map/broadcast_in_dim | solution.py:78
  55.4 10.2 %collective-permute-done = bf16[64,4096]{1,0:T(8,128)(2,1)S(1)} collective-permute-done((bf16[64,4096]{1,0:T(8,128)(2,1)S(1)}, bf16[64,4096]{1,0:T(8,128)(2,1)S(1)}, u32[]{:S(2)}, u32[]{:S(2)}) %collective-permute-start) | collective-permute-done | bytes 524320 | tf_op jit(solution)/shard_map/ppermute | solution.py:15
  65.7 0.8 %copy.33 = bf16[1,64,4096]{2,1,0:T(8,128)(2,1)} copy(bf16[1,64,4096]{2,1,0:T(8,128)(2,1)S(1)} %bitcast.83) | data formatting | bytes 1048576
  (5 shorter events, 0.1 us)
Async XLA Ops:
  0.6 20.5 %copy-start = (bf16[1,256,128]{2,1,0:T(8,128)(2,1)S(1)}, bf16[1,256,128]{2,1,0:T(8,128)(2,1)}, u32[]{:S(2)}) copy-start(bf16[1,256,128]{2,1,0:T(8,128)(2,1)} %param.6) | copy-start | bytes 196612
  52.3 13.4 %collective-permute-start = (bf16[64,4096]{1,0:T(8,128)(2,1)S(1)}, bf16[64,4096]{1,0:T(8,128)(2,1)S(1)}, u32[]{:S(2)}, u32[]{:S(2)}) collective-permute-start(bf16[64,4096]{1,0:T(8,128)(2,1)S(1)} %bitcast.84), channel_id=1, source_target_pairs={{16,0},{0,16},{17,1},{1,17},{18,2},{2,18},{19,3},{3,19},{20,4},{4,... | collective-permute-start | bytes 1572872 | tf_op jit(solution)/shard_map/ppermute | solution.py:15
where the time goes:
time: 66.7 us; the launch traced here: 66.4 us
  blocking collectives  41.7 us (63%)
  waiting for transfers between devices  10.2 us (15%)
  local copies, waits for them, and re-layouts  4.88 us (7%)
  matrix products  4 us (6%)
  other arithmetic  3.34 us (5%)
  starting transfers between devices  1.56 us (2%)
  between operations  0.73 us (1%)
    all_gather x1, blocking collectives, body(): key_piece = lax.all_gather(key_rows, 'ctx', axis=0, tiled=True)  15.8 us
    all_gather x1, blocking collectives, body(): value_piece = lax.all_gather(value_rows, 'ctx', axis=0, tiled=True)  14.4 us
    all_to_all x1, blocking collectives, body(): own = lax.all_to_all(result, 'mp', split_axis=0, concat_axis=1, tiled=True)  11.4 us
    ppermute x1, waiting for transfers between devices, from_behind(): return lax.ppermute(block, axis, route)  10.2 us
    dot_general x1, matrix products, body(): jnp.einsum('hgqk,khd->qhgd', weight.astype(jnp.bfloat16), value_piece.res...  2.64 us
    reduce_sum x1, other arithmetic, body(): total = jnp.sum(weight, axis=-1)  2 us
    unnamed x4, local copies, waits for them, and re-layouts  1.93 us
    ppermute x1, starting transfers between devices, from_behind(): return lax.ppermute(block, axis, route)  1.56 us
  transfers between devices with their start and end apart: 1, of which 1 were waited for; matrix products, arithmetic and copies ran while one was open for 2% of the time, Pallas kernels for 0%

commit v1 on v0

v1 whole, which is shorter than its diff:
```python
import functools
import math

import jax
import jax.numpy as jnp
from jax import lax
from jax.experimental import pallas as pl
from jax.experimental.pallas import tpu as pltpu
from jax.sharding import PartitionSpec as P

DH = 128
DOCS = 16
MESH = pl.DeviceIdType.MESH
LOG2E = 1.4426950408889634
GROUP = 2


def kernel(
    dims,
    q_hbm, k_hbm, v_hbm, lengths,
    own_hbm, moved_hbm,
    q, k, v, score, bias, result,
    load_sem, kv_send, kv_recv, row_send, row_recv, own_sem, pass_send, pass_recv,
):
    sections, cycle, split, rows, heads, hops = dims
    s, p, m = lax.axis_index("section"), lax.axis_index("ctx"), lax.axis_index("mp")
    after = lax.rem(s + 1, sections)
    width = heads * DH
    part = rows // split
    groups = heads // GROUP
    span = GROUP * DH

    def load(i):
        pairs = ((k_hbm.at[0], k.at[pl.ds(0, rows)]), (v_hbm.at[0], v.at[pl.ds(0, rows)]), (q_hbm.at[0], q))
        return pltpu.make_async_copy(*pairs[i], load_sem.at[i])

    def shift(d, i):
        buf, first = ((k, k_hbm), (v, v_hbm))[i]
        src = first.at[0] if d == 0 else buf.at[pl.ds(d * rows, rows)]
        return pltpu.make_async_remote_copy(
            src_ref=src,
            dst_ref=buf.at[pl.ds((d + 1) * rows, rows)],
            send_sem=kv_send.at[d, i],
            recv_sem=kv_recv.at[d, i],
            device_id={"ctx": p + 1},
            device_id_type=MESH,
        )

    def place(holder, g):
        return pl.ds(pl.multiple_of(holder * width + g * span, DH), span)

    def spread(g, i):
        to = lax.rem(m + i, split)
        return pltpu.make_async_remote_copy(
            src_ref=result.at[pl.ds(pl.multiple_of(to * part, 16), part), pl.ds(g * span, span)],
            dst_ref=own_hbm.at[0, :, place(m, g)],
            send_sem=row_send.at[g, i - 1],
            recv_sem=row_recv.at[g, i - 1],
            device_id={"mp": to},
            device_id_type=MESH,
        )

    def arrive(g, i):
        cols = place(lax.rem(m + split - i, split), g)
        return pltpu.make_async_remote_copy(
            src_ref=own_hbm.at[0, :, cols],
            dst_ref=own_hbm.at[0, :, cols],
            send_sem=row_send.at[g, i - 1],
            recv_sem=row_recv.at[g, i - 1],
            device_id={"mp": lax.rem(m + i, split)},
            device_id_type=MESH,
        )

    def own_rows(g):
        return result.at[pl.ds(pl.multiple_of(m * part, 16), part), pl.ds(g * span, span)]

    def keep(g):
        return pltpu.make_async_copy(own_rows(g), own_hbm.at[0, :, place(m, g)], own_sem.at[g])

    def hand(g, i):
        cols = place(lax.rem(m + split - i, split), g)
        return pltpu.make_async_remote_copy(
            src_ref=own_rows(g) if i == 0 else own_hbm.at[0, :, cols],
            dst_ref=moved_hbm.at[0, :, cols],
            send_sem=pass_send.at[g, i],
            recv_sem=pass_recv.at[g, i],
            device_id={"section": after},
            device_id_type=MESH,
        )

    for i in range(3):
        load(i).start()

    barrier = pltpu.get_barrier_semaphore()

    def greet(where):
        pl.semaphore_signal(barrier, inc=1, device_id=where, device_id_type=MESH)

    pl.when(p < cycle - 1)(lambda: greet({"ctx": p + 1}))
    pl.when(p > 0)(lambda: greet({"ctx": p - 1}))
    for i in range(1, split):
        greet({"mp": lax.rem(m + i, split)})
    greet({"section": after})
    met = split
    if sections > 2:
        greet({"section": lax.rem(s + sections - 1, sections)})
        met += 1
    inside = (p > 0) & (p < cycle - 1)
    pl.when(inside)(lambda: pl.semaphore_wait(barrier, met + 2))
    pl.when(jnp.logical_not(inside))(lambda: pl.semaphore_wait(barrier, met + 1))

    @pl.when(p < cycle - 1)
    def _():
        shift(0, 0).start()
        shift(0, 1).start()

    for d in range(1, hops + 1):
        @pl.when(p < d)
        def _(d=d):
            k[pl.ds(d * rows, rows), :] = jnp.zeros((rows, DH), k.dtype)
            v[pl.ds(d * rows, rows), :] = jnp.zeros((rows, DH), v.dtype)

    t = p * rows + lax.broadcasted_iota(jnp.int32, (rows, 1), 0)
    begin = jnp.zeros((rows, 1), jnp.int32)
    finish = jnp.full((rows, 1), rows * cycle, jnp.int32)
    end = jnp.int32(0)
    for j in range(DOCS):
        end = end + lengths[0, j]
        past = t >= end
        begin = jnp.where(past, end, begin)
        finish = jnp.where(past, finish, jnp.minimum(finish, end))
    length = (finish - begin).astype(jnp.float32)
    factor = jnp.maximum(1.0, jnp.log(length) / math.log(float(rows * cycle // 16))) * (
        LOG2E / math.sqrt(DH)
    )
    for d in range(hops + 1):
        u = (p - d) * rows + lax.broadcasted_iota(jnp.int32, (rows, rows), 1)
        bias[:, d * rows:(d + 1) * rows] = jnp.where((u >= begin) & (u <= t), 0.0, -1e30)

    load(2).wait()
    for d in range(hops + 1):
        if d == 0:
            load(0).wait()
            load(1).wait()
        else:
            @pl.when(p >= d)
            def _(d=d):
                shift(d - 1, 0).wait_recv()
                if d < hops:
                    pl.when(p < cycle - 1)(lambda: shift(d, 0).start())
                shift(d - 1, 1).wait_recv()
                if d < hops:
                    pl.when(p < cycle - 1)(lambda: shift(d, 1).start())

        def raw(h, _, d=d):
            q_h = q[:, pl.ds(pl.multiple_of(h * DH, DH), DH)]
            prod = lax.dot_general(
                q_h, k[pl.ds(d * rows, rows), :], (((1,), (1,)), ((), ())),
                preferred_element_type=jnp.float32,
            )
            score[h, :, pl.ds(d * rows, rows)] = prod + bias[:, d * rows:(d + 1) * rows]
            return 0

        lax.fori_loop(0, heads, raw, 0, unroll=hops <= 4)

    def attend(h):
        x = score[h]
        top = jnp.max(x, axis=1, keepdims=True)
        weight = jnp.exp2((x - top) * factor)
        total = jnp.sum(weight, axis=1, keepdims=True)
        out = jnp.dot(weight.astype(jnp.bfloat16), v[...], preferred_element_type=jnp.float32)
        result[:, h * DH:(h + 1) * DH] = (out * (1.0 / total)).astype(jnp.bfloat16)

    def relay(g):
        for i in range(1, split):
            arrive(g, i).wait_recv()
            hand(g, i).start()

    for g in range(groups):
        for h in range(g * GROUP, (g + 1) * GROUP):
            attend(h)
        for i in range(1, split):
            spread(g, i).start()
        hand(g, 0).start()
        keep(g).start()
        if g > 0:
            relay(g - 1)
    relay(groups - 1)

    for d in range(hops):
        @pl.when((p >= d) & (p < cycle - 1))
        def _(d=d):
            shift(d, 0).wait_send()
            shift(d, 1).wait_send()
    for g in range(groups):
        keep(g).wait()
        for i in range(1, split):
            spread(g, i).wait_send()
        for i in range(split):
            hand(g, i).wait_send()
            hand(g, i).wait_recv()


def body(sections, cycle, split, queries, keys, values, doc_lengths):
    rows, width = queries.shape[1:]
    heads = width // DH
    assert keys.shape[2] == DH
    hops = min(cycle - 1, cycle // 2)
    span = (hops + 1) * rows
    groups = heads // GROUP
    part = rows // split
    out = jax.ShapeDtypeStruct((1, part, width * split), jnp.bfloat16)
    dma = pltpu.SemaphoreType.DMA
    hbm = pl.BlockSpec(memory_space=pl.ANY)
    return pl.pallas_call(
        functools.partial(kernel, (sections, cycle, split, rows, heads, hops)),
        out_shape=(out, out),
        in_specs=[hbm, hbm, hbm, pl.BlockSpec(memory_space=pltpu.SMEM)],
        out_specs=(hbm, hbm),
        scratch_shapes=[
            pltpu.VMEM((rows, width), jnp.bfloat16),
            pltpu.VMEM((span, DH), jnp.bfloat16),
            pltpu.VMEM((span, DH), jnp.bfloat16),
            pltpu.VMEM((heads, rows, span), jnp.float32),
            pltpu.VMEM((rows, span), jnp.float32),
            pltpu.VMEM((rows, width), jnp.bfloat16),
            dma((3,)),
            dma((hops, 2)),
            dma((hops, 2)),
            dma((groups, split - 1)),
            dma((groups, split - 1)),
            dma((groups,)),
            dma((groups, split)),
            dma((groups, split)),
        ],
        compiler_params=pltpu.CompilerParams(
            collective_id=0, has_side_effects=True, vmem_limit_bytes=60 * 2**20
        ),
        name="packed_attention",
    )(queries, keys, values, doc_lengths)


def solution(mesh):
    sizes = (mesh.shape["section"], mesh.shape["ctx"], mesh.shape["mp"])
    return jax.shard_map(
        functools.partial(body, *sizes),
        mesh=mesh,
        in_specs=(
            P("section", "ctx", "mp"),
            P("section", "ctx", "mp"),
            P("section", "ctx", "mp"),
            P("section", None),
        ),
        out_specs=(P("section", ("ctx", "mp"), None), P("section", ("ctx", "mp"), None)),
        check_vma=False,
    )
```

time: 66.7 us -> 30.3 us (0.45)
  the two profiles are of different devices: /device:TPU:0 before, /device:TPU:24 now
where the time goes in v1:
time: 30.3 us; the launch traced here: 30.1 us
  Pallas kernels  26.8 us (88%)
  local copies, waits for them, and re-layouts  2.72 us (9%)
  between operations  0.65 us (2%)
    pallas_call x1, Pallas kernels, body(): pl.pallas_call(functools.partial(kernel, (sections, cycle, split, rows, h...  26.8 us
    unnamed x4, local copies, waits for them, and re-layouts  2.72 us

profile of v1, /device:TPU:24, one launch (start us, length us, event | category | flops | bytes accessed | tf_op | source)
XLA Modules:
  0.0 30.1 jit_solution(16155699693948967818)
XLA Ops:
  0.6 26.8 %packed_attention.1 = (bf16[1,64,4096]{2,1,0:T(8,128)(2,1)}, bf16[1,64,4096]{2,1,0:T(8,128)(2,1)}) custom-call(bf16[1,256,1024]{2,1,0:T(8,128)(2,1)} %q_hbm.1, bf16[1,256,128]{2,1,0:T(8,128)(2,1)} %k_hbm.1, bf16[1,256,128]{2,1,0:T(8,128)(2,1)} %v_hbm.1, s32[1,16]{1,0:T(1,128)} %lengths.1), custom_call_target="tpu_custom_call" | custom-call | tf_op jit(solution)/shard_map/packed_attention/pallas_call | solution.py:215
  27.4 0.0 copy-start
  27.4 1.9 %copy.8 = bf16[1,64,4096]{2,1,0:T(8,128)(2,1)} copy(bf16[1,64,4096]{2,1,0:T(8,128)(2,1)} %get-tuple-element.4) | data formatting | bytes 1048576
  29.3 0.0 copy-done
  29.3 0.8 %copy.9 = bf16[1,64,4096]{2,1,0:T(8,128)(2,1)} copy(bf16[1,64,4096]{2,1,0:T(8,128)(2,1)S(1)} %copy-done) | data formatting | bytes 1048576
Async XLA Ops:
  27.4 1.9 %copy-start = (bf16[1,64,4096]{2,1,0:T(8,128)(2,1)S(1)}, bf16[1,64,4096]{2,1,0:T(8,128)(2,1)}, u32[]{:S(2)}) copy-start(bf16[1,64,4096]{2,1,0:T(8,128)(2,1)} %get-tuple-element.5) | copy-start | bytes 1572868

commit v2 on v1

--- a/solution.py
+++ b/solution.py
@@ -60,17 +60,6 @@
             device_id_type=MESH,
         )
 
-    def arrive(g, i):
-        cols = place(lax.rem(m + split - i, split), g)
-        return pltpu.make_async_remote_copy(
-            src_ref=own_hbm.at[0, :, cols],
-            dst_ref=own_hbm.at[0, :, cols],
-            send_sem=row_send.at[g, i - 1],
-            recv_sem=row_recv.at[g, i - 1],
-            device_id={"mp": lax.rem(m + i, split)},
-            device_id_type=MESH,
-        )
-
     def own_rows(g):
         return result.at[pl.ds(pl.multiple_of(m * part, 16), part), pl.ds(g * span, span)]
 
@@ -78,13 +67,13 @@
         return pltpu.make_async_copy(own_rows(g), own_hbm.at[0, :, place(m, g)], own_sem.at[g])
 
     def hand(g, i):
-        cols = place(lax.rem(m + split - i, split), g)
+        to = lax.rem(m + i, split)
         return pltpu.make_async_remote_copy(
-            src_ref=own_rows(g) if i == 0 else own_hbm.at[0, :, cols],
-            dst_ref=moved_hbm.at[0, :, cols],
+            src_ref=result.at[pl.ds(pl.multiple_of(to * part, 16), part), pl.ds(g * span, span)],
+            dst_ref=moved_hbm.at[0, :, place(m, g)],
             send_sem=pass_send.at[g, i],
             recv_sem=pass_recv.at[g, i],
-            device_id={"section": after},
+            device_id={"section": after, "mp": to},
             device_id_type=MESH,
         )
 
@@ -100,11 +89,14 @@
     pl.when(p > 0)(lambda: greet({"ctx": p - 1}))
     for i in range(1, split):
         greet({"mp": lax.rem(m + i, split)})
-    greet({"section": after})
-    met = split
+    for i in range(split):
+        greet({"section": after, "mp": lax.rem(m + i, split)})
+    met = 2 * split - 1
     if sections > 2:
-        greet({"section": lax.rem(s + sections - 1, sections)})
-        met += 1
+        before = lax.rem(s + sections - 1, sections)
+        for i in range(split):
+            greet({"section": before, "mp": lax.rem(m + i, split)})
+        met += split
     inside = (p > 0) & (p < cycle - 1)
     pl.when(inside)(lambda: pl.semaphore_wait(barrier, met + 2))
     pl.when(jnp.logical_not(inside))(lambda: pl.semaphore_wait(barrier, met + 1))
@@ -171,21 +163,14 @@
         out = jnp.dot(weight.astype(jnp.bfloat16), v[...], preferred_element_type=jnp.float32)
         result[:, h * DH:(h + 1) * DH] = (out * (1.0 / total)).astype(jnp.bfloat16)
 
-    def relay(g):
-        for i in range(1, split):
-            arrive(g, i).wait_recv()
-            hand(g, i).start()
-
     for g in range(groups):
         for h in range(g * GROUP, (g + 1) * GROUP):
             attend(h)
+        for i in range(split):
+            hand(g, i).start()
         for i in range(1, split):
             spread(g, i).start()
-        hand(g, 0).start()
         keep(g).start()
-        if g > 0:
-            relay(g - 1)
-    relay(groups - 1)
 
     for d in range(hops):
         @pl.when((p >= d) & (p < cycle - 1))
@@ -196,6 +181,7 @@
         keep(g).wait()
         for i in range(1, split):
             spread(g, i).wait_send()
+            spread(g, i).wait_recv()
         for i in range(split):
             hand(g, i).wait_send()
             hand(g, i).wait_recv()
@@ -209,14 +195,14 @@
     span = (hops + 1) * rows
     groups = heads // GROUP
     part = rows // split
-    out = jax.ShapeDtypeStruct((1, part, width * split), jnp.bfloat16)
+    out = pltpu.VMEM((1, part, width * split), jnp.bfloat16)
     dma = pltpu.SemaphoreType.DMA
     hbm = pl.BlockSpec(memory_space=pl.ANY)
     return pl.pallas_call(
         functools.partial(kernel, (sections, cycle, split, rows, heads, hops)),
         out_shape=(out, out),
         in_specs=[hbm, hbm, hbm, pl.BlockSpec(memory_space=pltpu.SMEM)],
-        out_specs=(hbm, hbm),
+        out_specs=(pl.BlockSpec(memory_space=pltpu.VMEM),) * 2,
         scratch_shapes=[
             pltpu.VMEM((rows, width), jnp.bfloat16),
             pltpu.VMEM((span, DH), jnp.bfloat16),

time: 30.3 us -> 26.5 us (0.87)
  the two profiles are of different devices: /device:TPU:24 before, /device:TPU:29 now
where the time goes in v2:
time: 26.5 us; the launch traced here: 26.3 us
  Pallas kernels  24.1 us (91%)
  local copies, waits for them, and re-layouts  1.59 us (6%)
  between operations  0.64 us (2%)
    pallas_call x1, Pallas kernels, body(): pl.pallas_call(functools.partial(kernel, (sections, cycle, split, rows, h...  24.1 us
    unnamed x2, local copies, waits for them, and re-layouts  1.59 us

profile of v2, /device:TPU:29, one launch (start us, length us, event | category | flops | bytes accessed | tf_op | source)
XLA Modules:
  0.0 26.3 jit_solution(10279389925594750707)
XLA Ops:
  0.6 24.1 %packed_attention.1 = (bf16[1,64,4096]{2,1,0:T(8,128)(2,1)S(1)}, bf16[1,64,4096]{2,1,0:T(8,128)(2,1)S(1)}) custom-call(bf16[1,256,1024]{2,1,0:T(8,128)(2,1)} %q_hbm.1, bf16[1,256,128]{2,1,0:T(8,128)(2,1)} %k_hbm.1, bf16[1,256,128]{2,1,0:T(8,128)(2,1)} %v_hbm.1, s32[1,16]{1,0:T(1,128)} %lengths.1), custom_call_target="tpu_custom_call" | custom-call | tf_op jit(solution)/shard_map/packed_attention/pallas_call | solution.py:201
  24.7 0.8 %copy.8 = bf16[1,64,4096]{2,1,0:T(8,128)(2,1)} copy(bf16[1,64,4096]{2,1,0:T(8,128)(2,1)S(1)} %get-tuple-element.2) | data formatting | bytes 1048576
  25.5 0.8 %copy.9 = bf16[1,64,4096]{2,1,0:T(8,128)(2,1)} copy(bf16[1,64,4096]{2,1,0:T(8,128)(2,1)S(1)} %get-tuple-element.3) | data formatting | bytes 1048576

commit v3 on v2

--- a/solution.py
+++ b/solution.py
@@ -12,14 +12,14 @@
 DOCS = 16
 MESH = pl.DeviceIdType.MESH
 LOG2E = 1.4426950408889634
-GROUP = 2
+GROUP = 4
 
 
 def kernel(
     dims,
     q_hbm, k_hbm, v_hbm, lengths,
     own_hbm, moved_hbm,
-    q, k, v, score, bias, result,
+    q, k, v, score, soft, bias, result,
     load_sem, kv_send, kv_recv, row_send, row_recv, own_sem, pass_send, pass_recv,
 ):
     sections, cycle, split, rows, heads, hops = dims
@@ -129,39 +129,51 @@
         u = (p - d) * rows + lax.broadcasted_iota(jnp.int32, (rows, rows), 1)
         bias[:, d * rows:(d + 1) * rows] = jnp.where((u >= begin) & (u <= t), 0.0, -1e30)
 
+    staged = hops <= 4
     load(2).wait()
-    for d in range(hops + 1):
-        if d == 0:
-            load(0).wait()
-            load(1).wait()
-        else:
+    load(0).wait()
+    load(1).wait()
+
+    def raw(h, d, count):
+        prod = lax.dot_general(
+            q[:, h * DH:(h + 1) * DH], k[pl.ds(d * rows, count * rows), :], (((1,), (1,)), ((), ())),
+            preferred_element_type=jnp.float32,
+        )
+        return prod + bias[:, d * rows:(d + count) * rows]
+
+    def ready(d, i):
+        if d > 0:
             @pl.when(p >= d)
-            def _(d=d):
-                shift(d - 1, 0).wait_recv()
+            def _():
+                shift(d - 1, i).wait_recv()
                 if d < hops:
-                    pl.when(p < cycle - 1)(lambda: shift(d, 0).start())
-                shift(d - 1, 1).wait_recv()
-                if d < hops:
-                    pl.when(p < cycle - 1)(lambda: shift(d, 1).start())
-
-        def raw(h, _, d=d):
-            q_h = q[:, pl.ds(pl.multiple_of(h * DH, DH), DH)]
-            prod = lax.dot_general(
-                q_h, k[pl.ds(d * rows, rows), :], (((1,), (1,)), ((), ())),
-                preferred_element_type=jnp.float32,
-            )
-            score[h, :, pl.ds(d * rows, rows)] = prod + bias[:, d * rows:(d + 1) * rows]
-            return 0
-
-        lax.fori_loop(0, heads, raw, 0, unroll=hops <= 4)
-
-    def attend(h):
-        x = score[h]
+                    pl.when(p < cycle - 1)(lambda: shift(d, i).start())
+
+    def soften(x):
         top = jnp.max(x, axis=1, keepdims=True)
         weight = jnp.exp2((x - top) * factor)
-        total = jnp.sum(weight, axis=1, keepdims=True)
-        out = jnp.dot(weight.astype(jnp.bfloat16), v[...], preferred_element_type=jnp.float32)
-        result[:, h * DH:(h + 1) * DH] = (out * (1.0 / total)).astype(jnp.bfloat16)
+        return weight.astype(jnp.bfloat16), 1.0 / jnp.sum(weight, axis=1, keepdims=True)
+
+    inverse = []
+    for d in range(hops + 1):
+        ready(d, 0)
+        if staged and d < hops:
+            for h in range(heads):
+                score[h, :, d * rows:(d + 1) * rows] = raw(h, d, 1)
+        if staged and d == hops:
+            for h in range(heads):
+                x = jnp.concatenate([score[h], raw(h, d, 1)], axis=1)
+                soft[h], over = soften(x)
+                inverse.append(over)
+        ready(d, 1)
+
+    def attend(h):
+        if staged:
+            weight, over = soft[h], inverse[h]
+        else:
+            weight, over = soften(raw(h, 0, hops + 1))
+        out = jnp.dot(weight, v[...], preferred_element_type=jnp.float32)
+        result[:, h * DH:(h + 1) * DH] = (out * over).astype(jnp.bfloat16)
 
     for g in range(groups):
         for h in range(g * GROUP, (g + 1) * GROUP):
@@ -207,7 +219,8 @@
             pltpu.VMEM((rows, width), jnp.bfloat16),
             pltpu.VMEM((span, DH), jnp.bfloat16),
             pltpu.VMEM((span, DH), jnp.bfloat16),
-            pltpu.VMEM((heads, rows, span), jnp.float32),
+            pltpu.VMEM((heads, rows, span - rows) if hops <= 4 else (8, DH), jnp.float32),
+            pltpu.VMEM((heads, rows, span) if hops <= 4 else (16, DH), jnp.bfloat16),
             pltpu.VMEM((rows, span), jnp.float32),
             pltpu.VMEM((rows, width), jnp.bfloat16),
             dma((3,)),

time: 26.5 us -> 26 us (0.981)
  Pallas kernels: 24.1 us -> 23.5 us
    pallas_call x1, Pallas kernels: 24.1 us -> 23.5 us  [body(): pl.pallas_call(functools.partial(kernel, (sections, cycle, split, rows, h...]
where the time goes in v3:
time: 26 us; the launch traced here: 25.8 us
  Pallas kernels  23.5 us (90%)
  local copies, waits for them, and re-layouts  1.59 us (6%)
  between operations  0.64 us (2%)
    pallas_call x1, Pallas kernels, body(): pl.pallas_call(functools.partial(kernel, (sections, cycle, split, rows, h...  23.5 us
    unnamed x2, local copies, waits for them, and re-layouts  1.59 us

profile of v3, /device:TPU:29, one launch (start us, length us, event | category | flops | bytes accessed | tf_op | source)
XLA Modules:
  0.0 25.8 jit_solution(13981674562280394728)
XLA Ops:
  0.6 23.5 %packed_attention.1 = (bf16[1,64,4096]{2,1,0:T(8,128)(2,1)S(1)}, bf16[1,64,4096]{2,1,0:T(8,128)(2,1)S(1)}) custom-call(bf16[1,256,1024]{2,1,0:T(8,128)(2,1)} %q_hbm.1, bf16[1,256,128]{2,1,0:T(8,128)(2,1)} %k_hbm.1, bf16[1,256,128]{2,1,0:T(8,128)(2,1)} %v_hbm.1, s32[1,16]{1,0:T(1,128)} %lengths.1), custom_call_target="tpu_custom_call" | custom-call | tf_op jit(solution)/shard_map/packed_attention/pallas_call | solution.py:213
  24.2 0.8 %copy.8 = bf16[1,64,4096]{2,1,0:T(8,128)(2,1)} copy(bf16[1,64,4096]{2,1,0:T(8,128)(2,1)S(1)} %get-tuple-element.2) | data formatting | bytes 1048576
  25.0 0.8 %copy.9 = bf16[1,64,4096]{2,1,0:T(8,128)(2,1)} copy(bf16[1,64,4096]{2,1,0:T(8,128)(2,1)S(1)} %get-tuple-element.3) | data formatting | bytes 1048576
